TPU v7x, 32 devices: a whole 2x2x4 slice. The times are simulated.
32 devices in a mesh: sub: 16 (over z, y, x), crs: 2 (over core).
Axes of the slice: x: 2, y: 2, z: 4, core: 2. Of those that a mesh axis runs over, the one named last changes fastest.
Arguments:
- right_side: float32 [4, 16, 2, 384], P(None, 'sub', 'crs'), may hold values from -40 to 40
- own_block: bfloat16 [16, 2, 384, 384], P('sub', 'crs'), may hold values from -1 to 3
- coupling: bfloat16 [16, 2, 384, 768], P('sub', 'crs'), may hold values from -0.1875 to 0.1875
- local_inverse: bfloat16 [16, 2, 384, 1152], P('sub', 'crs'), may hold values from -1 to 3
- coarse_basis: float32 [16, 2, 40, 384], P('sub', 'crs'), may hold values from -0.3125 to 0.3125
- coarse_inverse: bfloat16 [16, 80, 2, 640], P('sub', None, 'crs'), may hold values from -1 to 4
- neighbours: int32 [16, 2, 6], P('sub', 'crs'), may hold values from 0 to 15, as said below
- margin_rows: int32 [16, 2, 6, 128], P('sub', 'crs'), may hold values from 0 to 383, as said below
- block_counts: int32 [16, 2], P('sub', 'crs'), may hold values from 4 to 6, as said below
Outputs:
- solution: float32 [4, 16, 2, 384], P(None, 'sub', 'crs')
- basis_next: float32 [4, 16, 2, 384], P(None, 'sub', 'crs')
Inputs may be any that keep to these rules, and one draw needn't show every extreme that they name: A subdomain's listed neighbours are distinct sub indices other than its own; slot j of (s, c) names subdomain (neighbours[s, c, j], c). `margin_rows`: the rows of one block are distinct. `block_counts`: some subdomain uses all 6 slots.
All inputs are finite; a program needn't handle non-finite values.
Results may differ from a plain program's by a relative error of at most 0.0095.
Values may be sent and summed in bfloat16 or wider, within the bound.
A program may use at most 64 MiB of HBM per device.

v0:
```python
import functools

import jax
import jax.numpy as jnp
from jax import lax
from jax.experimental import pallas as pl
from jax.experimental.pallas import tpu as pltpu
from jax.sharding import PartitionSpec as P

EPSILON = 1e-06
MESH = pl.DeviceIdType.MESH
LANES = 128
ROUNDS = 4
SHARES = 2
AT = 120
NT = (((1,), (1,)), ((), ()))
LOW = jnp.bfloat16
WIDE = jnp.float32


def least_squares(start_norm, columns):
    cosines = []
    sine_terms = []
    triangle = []
    target = [start_norm] + [jnp.zeros_like(start_norm) for j in range(len(columns))]
    for j, column in enumerate(columns):
        column = list(column)
        for i in range(j):
            upper_value = cosines[i] * column[i] + sine_terms[i] * column[i + 1]
            column[i + 1] = -sine_terms[i] * column[i] + cosines[i] * column[i + 1]
            column[i] = upper_value
        radius = jnp.sqrt(column[j] * column[j] + column[j + 1] * column[j + 1])
        cosine = column[j] / radius
        sine_part = column[j + 1] / radius
        column[j] = radius
        target[j + 1] = -sine_part * target[j]
        target[j] = cosine * target[j]
        cosines.append(cosine)
        sine_terms.append(sine_part)
        triangle.append(column[: j + 1])
    weights = [None] * len(columns)
    for j in reversed(range(len(columns))):
        running = target[j]
        for k in range(j + 1, len(columns)):
            running = running - triangle[k][j] * weights[k]
        weights[j] = running / triangle[j][j]
    return weights


def kernel(
    sizes,
    right_hbm,
    own_hbm,
    couple_hbm,
    inverse_hbm,
    basis_hbm,
    coarse_hbm,
    listed_hbm,
    picked_hbm,
    counts_hbm,
    both_ref,
    right_ref,
    own_ref,
    couple_ref,
    inverse_ref,
    basis_ref,
    coarse_ref,
    listed_ref,
    picked_ref,
    counts_ref,
    sent,
    held_0,
    held_1,
    held_2,
    held_3,
    share,
    last_rows,
    pick,
    coarse_wide,
    placed,
    basis_parts,
    shifted,
    shifted_parts,
    load_sems,
    send_sem,
    recv_sems,
    share_send_sem,
    share_sems,
    last_send_sem,
    last_sem,
):
    subs, crs, cols, rows, kc, slots, share_lanes, together, groups = sizes
    held = (held_0, held_1, held_2, held_3)
    me = lax.axis_index("sub")
    mine = lax.axis_index("crs")
    all_rows = float(rows * subs * crs)
    row_of = lax.broadcasted_iota(jnp.int32, (8, LANES), 0)
    lane_of = lax.broadcasted_iota(jnp.int32, (8, LANES), 1)
    top = row_of < 4

    pairs = [
        (right_hbm, right_ref),
        (basis_hbm, basis_ref),
        (picked_hbm, picked_ref),
        (counts_hbm, counts_ref),
        (coarse_hbm, coarse_ref),
        (listed_hbm, listed_ref),
        (inverse_hbm, inverse_ref),
        (own_hbm, own_ref),
        (couple_hbm, couple_ref),
    ]
    loads = [
        pltpu.make_async_copy(there, here, load_sems.at[n])
        for n, (there, here) in enumerate(pairs)
    ]
    for load in loads:
        load.start()
    barrier = pltpu.get_barrier_semaphore()

    def greet_sub(i, carry):
        pl.semaphore_signal(
            barrier, inc=1, device_id=(lax.rem(me + i, subs), mine), device_id_type=MESH
        )
        return carry

    def greet_crs(i, carry):
        pl.semaphore_signal(
            barrier, inc=1, device_id=(me, lax.rem(mine + i, crs)), device_id_type=MESH
        )
        return carry

    lax.fori_loop(1, subs, greet_sub, 0)
    lax.fori_loop(1, crs, greet_crs, 0)


    def swap_halves(block):
        return pltpu.roll(block, 4, 0)

    def stack_parts(block):
        width = block.shape[1]
        high = block.astype(LOW).astype(WIDE)
        low = block - high
        at_top = lax.broadcasted_iota(jnp.int32, (8, width), 0) < 4
        return jnp.where(at_top, high, pltpu.roll(low, 4, 0)).astype(LOW)

    def nt(a, b):
        return lax.dot_general(a, b, NT, preferred_element_type=WIDE)

    def nn(a, b):
        return jnp.dot(a, b, preferred_element_type=WIDE)

    def row_sum(a):
        return jnp.sum(a, axis=1, keepdims=True)

    def restrict(block):
        parts = stack_parts(block)
        both = nt(parts, basis_parts[0]) + nt(parts, basis_parts[1])
        return both + swap_halves(both)

    def encode(value):
        high = value.astype(LOW).astype(WIDE)
        rest = value - high
        middle = rest.astype(LOW).astype(WIDE)
        low = rest - middle
        spread = jnp.where(lane_of == AT, high, 0.0)
        spread = jnp.where(lane_of == AT + 1, middle, spread)
        return jnp.where(lane_of == AT + 2, low, spread)

    def pack(block, extra):
        first = jnp.where(top, block[:, :LANES], swap_halves(block[:, LANES : 2 * LANES]))
        second = jnp.where(top, block[:, 2 * LANES :], swap_halves(extra))
        return jnp.concatenate([first, second], axis=0).astype(LOW)

    def send(number, tile):
        sent[number] = tile

        def one(i, carry):
            pltpu.make_async_remote_copy(
                src_ref=sent.at[number],
                dst_ref=held[number].at[me],
                send_sem=send_sem,
                recv_sem=recv_sems.at[number],
                device_id=(lax.rem(me + i, subs), mine),
                device_id_type=MESH,
            ).start()
            return carry

        lax.fori_loop(1, subs, one, 0)

    def receive(number):
        arrived = held[number].at[pl.ds(0, subs - 1)]
        pltpu.make_async_copy(arrived, arrived, recv_sems.at[number]).wait()

    def send_share(number, block):
        share[number, mine] = block

        def one(i, carry):
            pltpu.make_async_remote_copy(
                src_ref=share.at[number, mine],
                dst_ref=share.at[number, mine],
                send_sem=share_send_sem,
                recv_sem=share_sems.at[number],
                device_id=(me, lax.rem(mine + i, crs)),
                device_id_type=MESH,
            ).start()
            return carry

        lax.fori_loop(1, crs, one, 0)

    def receive_share(number):
        arrived = share.at[number, pl.ds(0, crs - 1)]
        pltpu.make_async_copy(arrived, arrived, share_sems.at[number]).wait()
        total = share[number, 0]
        for c in range(1, crs):
            total = total + share[number, c]
        return total

    def margin(number):
        lines = []
        for j in range(slots):
            tile = held[number][listed_ref[0, 0, j]].astype(WIDE)
            first = tile[:8]
            lines.append(jnp.concatenate([first, swap_halves(first), tile[8:]], axis=1))
        fetched = nn(jnp.concatenate(lines, axis=0).astype(LOW), pick[...])
        parts = [
            fetched[8 * j : 8 * j + 8, LANES * j : LANES * j + LANES] for j in range(slots)
        ]
        return jnp.concatenate(parts, axis=1).astype(LOW)

    def group_sums(number):
        sums = []
        for g in range(groups):
            members = range(g * together, min(subs, (g + 1) * together))
            tiles = [held[number][s].astype(WIDE)[8:] for s in members]
            sums.append(functools.reduce(jnp.add, tiles))
        return sums

    def with_scalars(solved, totals):
        if share_lanes > LANES:
            totals = jnp.concatenate(
                [totals, jnp.zeros((8, share_lanes - LANES), WIDE)], axis=1
            )
        at_top = lax.broadcasted_iota(jnp.int32, (8, share_lanes), 0) < 4
        return jnp.where(at_top, pltpu.roll(solved, 4, 0), totals)

    def scalar(block):
        return row_sum(jnp.where((lane_of >= AT) & (lane_of < AT + 3), block, 0.0))

    def prolong(total):
        parts = stack_parts(total)
        both = nn(parts, shifted_parts[0]) + nn(parts, shifted_parts[1])
        return both + pltpu.roll(both, 4, 0)

    def precondition(number, share_number, own_part):
        receive(number)
        sums = group_sums(number)
        solved = nt(jnp.concatenate(sums, axis=1).astype(LOW), coarse_wide[...])
        totals = functools.reduce(jnp.add, sums)
        send_share(share_number, with_scalars(solved, totals))
        fine = own_part + nt(margin(number), inverse_ref[:, rows:])
        total = receive_share(share_number)
        return fine + prolong(total), swap_halves(total[:, :LANES])

    loads[0].wait()
    loads[1].wait()
    right = jnp.concatenate(
        [right_ref[q] for q in range(cols)] + [jnp.zeros((8 - cols, rows), WIDE)], axis=0
    )
    basis = basis_ref[0, 0]
    placed[...] = jnp.zeros_like(placed)
    placed[pl.ds(pl.multiple_of(lax.rem(me, together) * kc, 8), kc), :] = basis
    basis_full = placed[...]
    basis_high = basis_full.astype(LOW)
    basis_parts[0] = basis_high
    basis_parts[1] = (basis_full - basis_high.astype(WIDE)).astype(LOW)
    extra = restrict(right) + encode(row_sum(right * right))
    tile = pack(right, extra)
    held_0[me] = tile
    pl.semaphore_wait(barrier, subs - 1 + crs - 1)
    send(0, tile)

    loads[2].wait()
    loads[3].wait()
    live = lax.broadcasted_iota(jnp.int32, (slots, LANES), 0) < counts_ref[0, 0]
    wanted = jnp.where(
        live, jnp.concatenate([picked_ref[0, j] for j in range(slots)], axis=0), -1
    )
    row_index = lax.broadcasted_iota(jnp.int32, (rows, LANES), 0)
    for j in range(slots):
        pick[:, j * LANES : (j + 1) * LANES] = jnp.where(
            row_index == wanted[j : j + 1], 1.0, 0.0
        ).astype(LOW)
    shifted[...] = jnp.zeros_like(shifted)
    shifted[pl.ds(pl.multiple_of(mine * kc, 8), kc), :] = basis
    shifted_full = shifted[...]
    shifted_high = shifted_full.astype(LOW)
    shifted_parts[0] = shifted_high
    shifted_parts[1] = (shifted_full - shifted_high.astype(WIDE)).astype(LOW)
    loads[4].wait()
    coarse_rows = crs * kc
    coarse_cols = subs * kc
    coarse_wide[...] = jnp.zeros_like(coarse_wide)
    coarse_lane = lax.broadcasted_iota(jnp.int32, (coarse_rows, LANES), 1)
    for g in range(groups):
        first = g * together * kc
        count = min(together * kc, coarse_cols - first)
        base = first // LANES * LANES
        offset = first - base
        width = LANES if offset + count <= LANES else 2 * LANES
        window = coarse_ref[:, base : base + width].astype(WIDE)
        if offset:
            window = pltpu.roll(window, width - offset, 1)
        coarse_wide[:coarse_rows, g * LANES : (g + 1) * LANES] = jnp.where(
            coarse_lane < count, window[:, :LANES], 0.0
        ).astype(LOW)
    loads[5].wait()
    loads[6].wait()
    own_fine = nt(right.astype(LOW), inverse_ref[:, :rows])

    first_z, totals = precondition(0, 0, own_fine)
    right_square = scalar(totals) / all_rows
    start = jnp.sqrt(right_square + EPSILON)

    nothing = jnp.zeros((8, LANES), WIDE)
    send(1, pack(first_z, nothing))
    loads[7].wait()
    loads[8].wait()
    own_part = nt(first_z.astype(LOW), own_ref[...])
    receive(1)
    mapped = own_part + nt(margin(1), couple_ref[...])

    extra = restrict(mapped) + encode(row_sum(mapped * right))
    tile = pack(mapped, extra)
    held_2[me] = tile
    send(2, tile)
    own_fine = nt(mapped.astype(LOW), inverse_ref[:, :rows])
    mapped_z, totals = precondition(2, 1, own_fine)
    height_11 = scalar(totals) / all_rows / (start * start)
    second_z = mapped_z - height_11 * first_z
    second = mapped - height_11 * right

    send(3, pack(second_z, nothing))
    own_part = nt(second_z.astype(LOW), own_ref[...])
    products = [row_sum(second * second), row_sum(right * second)]
    receive(3)
    last = own_part + nt(margin(3), couple_ref[...])

    products = products + [row_sum(last * right), row_sum(last * second), row_sum(last * last)]
    line = jnp.zeros((8, LANES), WIDE)
    for d, value in enumerate(products):
        line = jnp.where((lane_of == d * 4 + row_of) & top, value, line)
    here = me * crs + mine
    everyone = subs * crs
    last_rows[here] = jnp.sum(line, axis=0, keepdims=True)

    def send_last(i, carry):
        there = lax.rem(here + i, everyone)
        pltpu.make_async_remote_copy(
            src_ref=last_rows.at[here],
            dst_ref=last_rows.at[here],
            send_sem=last_send_sem,
            recv_sem=last_sem,
            device_id=(there // crs, lax.rem(there, crs)),
            device_id_type=MESH,
        ).start()
        return carry

    lax.fori_loop(1, everyone, send_last, 0)
    arrived = last_rows.at[pl.ds(0, everyone - 1)]
    pltpu.make_async_copy(arrived, arrived, last_sem).wait()
    whole = jnp.broadcast_to(jnp.sum(last_rows[...], axis=0), (8, LANES)) / all_rows

    def final(d):
        return row_sum(jnp.where(lane_of == d * 4 + row_of, whole, 0.0))

    second_square = final(0)
    length_1 = jnp.sqrt(second_square / (start * start) + EPSILON)
    scale = 1.0 / (start * length_1)
    start_scale = 1.0 / start
    gram_11 = right_square * start_scale * start_scale
    gram_12 = final(1) * start_scale * scale
    gram_22 = second_square * scale * scale
    height_12 = final(2) * start_scale * scale
    height_22 = final(3) * scale * scale
    last_square = final(4) * scale * scale
    rest = (
        last_square
        - height_12 * height_12 * (2.0 - gram_11)
        - height_22 * height_22 * (2.0 - gram_22)
        + 2.0 * height_12 * height_22 * gram_12
    )
    length_2 = jnp.sqrt(jnp.maximum(rest, 0.0) + EPSILON)
    weights = least_squares(start, [[height_11, length_1], [height_12, height_22, length_2]])
    result = (weights[0] * start_scale) * first_z + (weights[1] * scale) * second_z
    following = (last * scale - (height_12 * start_scale) * right - (height_22 * scale) * second) / length_2
    for q in range(cols):
        both_ref[0, q] = result[q : q + 1]
        both_ref[1, q] = following[q : q + 1]

    for number in range(ROUNDS):
        gone = held[number].at[pl.ds(0, subs - 1)]
        pltpu.make_async_copy(gone, gone, send_sem).wait()
    for number in range(SHARES):
        gone = share.at[number, pl.ds(0, crs - 1)]
        pltpu.make_async_copy(gone, gone, share_send_sem).wait()
    pltpu.make_async_copy(arrived, arrived, last_send_sem).wait()


def body(
    right_side,
    own_block,
    coupling,
    local_inverse,
    coarse_basis,
    coarse_inverse,
    neighbours,
    margin_rows,
    block_counts,
):
    cols, rows = right_side.shape[0], right_side.shape[3]
    subs, crs = lax.axis_size("sub"), lax.axis_size("crs")
    kc = coarse_basis.shape[2]
    slots, block_rows = margin_rows.shape[2:]
    coarse_rows = crs * kc
    share_lanes = -(-coarse_rows // LANES) * LANES
    together = (LANES - 8) // kc
    groups = -(-subs // together)
    sizes = (subs, crs, cols, rows, kc, slots, share_lanes, together, groups)
    vmem = pl.BlockSpec(memory_space=pltpu.VMEM)
    stays = pl.BlockSpec(memory_space=pltpu.HBM)
    both = pl.pallas_call(
        functools.partial(kernel, sizes),
        out_shape=jax.ShapeDtypeStruct((2, cols, 1, rows), WIDE),
        in_specs=[stays] * 9,
        out_specs=vmem,
        scratch_shapes=[
            pltpu.VMEM((cols, 1, rows), WIDE),
            pltpu.VMEM((rows, rows), LOW),
            pltpu.VMEM((rows, slots * block_rows), LOW),
            pltpu.VMEM((rows, rows + slots * block_rows), LOW),
            pltpu.VMEM((1, 1, kc, rows), WIDE),
            pltpu.VMEM((coarse_rows, subs * kc), LOW),
            pltpu.SMEM((1, 1, slots), jnp.int32),
            pltpu.VMEM((1, slots, 1, block_rows), jnp.int32),
            pltpu.SMEM((1, 1), jnp.int32),
            pltpu.VMEM((ROUNDS, 16, LANES), LOW),
            *[pltpu.VMEM((subs, 16, LANES), LOW) for number in range(ROUNDS)],
            pltpu.VMEM((SHARES, crs, 8, share_lanes), WIDE),
            pltpu.VMEM((subs * crs, 1, LANES), WIDE),
            pltpu.VMEM((rows, slots * block_rows), LOW),
            pltpu.VMEM((share_lanes, groups * LANES), LOW),
            pltpu.VMEM((LANES, rows), WIDE),
            pltpu.VMEM((2, LANES, rows), LOW),
            pltpu.VMEM((share_lanes, rows), WIDE),
            pltpu.VMEM((2, share_lanes, rows), LOW),
            pltpu.SemaphoreType.DMA((9,)),
            pltpu.SemaphoreType.DMA,
            pltpu.SemaphoreType.DMA((ROUNDS,)),
            pltpu.SemaphoreType.DMA,
            pltpu.SemaphoreType.DMA((SHARES,)),
            pltpu.SemaphoreType.DMA,
            pltpu.SemaphoreType.DMA,
        ],
        compiler_params=pltpu.CompilerParams(
            collective_id=0, has_side_effects=True, vmem_limit_bytes=63 * 1024 * 1024
        ),
    )(
        right_side.reshape(cols, 1, rows),
        own_block.reshape(rows, -1),
        coupling.reshape(rows, -1),
        local_inverse.reshape(rows, -1),
        coarse_basis,
        coarse_inverse.reshape(coarse_rows, -1),
        neighbours,
        margin_rows.reshape(1, slots, 1, block_rows),
        block_counts,
    )
    shape = (cols, 1, 1, rows)
    return both[0].reshape(shape), both[1].reshape(shape)


def solution(mesh):
    in_specs = (
        P(None, "sub", "crs", None),
        P("sub", "crs", None, None),
        P("sub", "crs", None, None),
        P("sub", "crs", None, None),
        P("sub", "crs", None, None),
        P("sub", None, "crs", None),
        P("sub", "crs", None),
        P("sub", "crs", None, None),
        P("sub", "crs"),
    )
    out_specs = (P(None, "sub", "crs", None), P(None, "sub", "crs", None))
    return jax.shard_map(body, mesh=mesh, in_specs=in_specs, out_specs=out_specs, check_vma=False)
```

profile of v0, /device:TPU:0, one launch (start us, length us, event | category | flops | bytes accessed | tf_op | source)
XLA Modules:
  0.0 36.2 jit_solution(17143785303400991933)
XLA Ops:
  1.3 33.6 %shard_map.104 = f32[2,4,1,384]{3,2,1,0:T(1,128)} custom-call(f32[4,1,384]{2,1,0:T(1,128)} %bitcast.18, bf16[384,384]{1,0:T(8,128)(2,1)} %bitcast.16, bf16[384,768]{1,0:T(8,128)(2,1)} %bitcast.15, bf16[384,1152]{1,0:T(8,128)(2,1)} %bitcast.14, f32[1,1,40,384]{3,2,1,0:T(8,128)} %basis_hbm.1, bf16[80,640]{1,0:T(8,128)(2,1)} %bitcast.17, ...), custom_call_target="tpu_custom_call" | custom-call | tf_op jit(solution)/shard_map/pallas_call | solution.py:431
  34.9 1.3 %slice_bitcast_fusion = (f32[4,1,1,384]{3,2,1,0:T(1,128)}, f32[4,1,1,384]{3,2,1,0:T(1,128)}) fusion(f32[2,4,1,384]{3,2,1,0:T(1,128)} %shard_map.104), kind=kLoop, calls=%fused_computation | loop fusion | bytes 24576
where the time goes:
time: 36.4 us; the launch traced here: 36.2 us
  Pallas kernels  33.6 us (92%)
  local copies, waits for them, and re-layouts  1.31 us (4%)
  between operations  1.29 us (4%)
    pallas_call x1, Pallas kernels, body(): pl.pallas_call(functools.partial(kernel, sizes), out_shape=jax.ShapeDtype...  33.6 us
    unnamed x1, local copies, waits for them, and re-layouts  1.31 us

commit v1 on v0

--- a/solution.py
+++ b/solution.py
@@ -12,6 +12,7 @@
 LANES = 128
 ROUNDS = 4
 SHARES = 2
+ORDER = (15, 11, 14, 13, 10, 9, 12, 8, 7, 6, 5, 4, 3, 2, 1)
 AT = 120
 NT = (((1,), (1,)), ((), ()))
 LOW = jnp.bfloat16
@@ -98,6 +99,46 @@
     lane_of = lax.broadcasted_iota(jnp.int32, (8, LANES), 1)
     top = row_of < 4
 
+    barrier = pltpu.get_barrier_semaphore()
+
+    short = subs & (subs - 1) == 0 and subs <= 16
+
+    def flipped(index, mask, bits):
+        moved = index
+        for k in range(bits):
+            if mask >> k & 1:
+                moved = moved + (1 << k) - (index // (1 << k)) % 2 * (2 << k)
+        return moved
+
+    def each_sub(act):
+        if short:
+            for mask in ORDER:
+                if mask < subs:
+                    act(flipped(me, mask, 4))
+        else:
+
+            def one(i, carry):
+                act(lax.rem(me + i, subs))
+                return carry
+
+            lax.fori_loop(1, subs, one, 0)
+
+    def each_crs(act):
+        def one(i, carry):
+            act(lax.rem(mine + i, crs))
+            return carry
+
+        if crs == 2:
+            act(1 - mine)
+        else:
+            lax.fori_loop(1, crs, one, 0)
+
+    def greet(sub, core):
+        pl.semaphore_signal(barrier, inc=1, device_id=(sub, core), device_id_type=MESH)
+
+    each_sub(lambda sub: greet(sub, mine))
+    each_crs(lambda core: greet(me, core))
+
     pairs = [
         (right_hbm, right_ref),
         (basis_hbm, basis_ref),
@@ -115,23 +156,6 @@
     ]
     for load in loads:
         load.start()
-    barrier = pltpu.get_barrier_semaphore()
-
-    def greet_sub(i, carry):
-        pl.semaphore_signal(
-            barrier, inc=1, device_id=(lax.rem(me + i, subs), mine), device_id_type=MESH
-        )
-        return carry
-
-    def greet_crs(i, carry):
-        pl.semaphore_signal(
-            barrier, inc=1, device_id=(me, lax.rem(mine + i, crs)), device_id_type=MESH
-        )
-        return carry
-
-    lax.fori_loop(1, subs, greet_sub, 0)
-    lax.fori_loop(1, crs, greet_crs, 0)
-
 
     def swap_halves(block):
         return pltpu.roll(block, 4, 0)
@@ -174,18 +198,17 @@
     def send(number, tile):
         sent[number] = tile
 
-        def one(i, carry):
+        def one(sub):
             pltpu.make_async_remote_copy(
                 src_ref=sent.at[number],
                 dst_ref=held[number].at[me],
                 send_sem=send_sem,
                 recv_sem=recv_sems.at[number],
-                device_id=(lax.rem(me + i, subs), mine),
+                device_id=(sub, mine),
                 device_id_type=MESH,
             ).start()
-            return carry
-
-        lax.fori_loop(1, subs, one, 0)
+
+        each_sub(one)
 
     def receive(number):
         arrived = held[number].at[pl.ds(0, subs - 1)]
@@ -194,18 +217,17 @@
     def send_share(number, block):
         share[number, mine] = block
 
-        def one(i, carry):
+        def one(core):
             pltpu.make_async_remote_copy(
                 src_ref=share.at[number, mine],
                 dst_ref=share.at[number, mine],
                 send_sem=share_send_sem,
                 recv_sem=share_sems.at[number],
-                device_id=(me, lax.rem(mine + i, crs)),
+                device_id=(me, core),
                 device_id_type=MESH,
             ).start()
-            return carry
-
-        lax.fori_loop(1, crs, one, 0)
+
+        each_crs(one)
 
     def receive_share(number):
         arrived = share.at[number, pl.ds(0, crs - 1)]
@@ -281,7 +303,7 @@
 
     loads[2].wait()
     loads[3].wait()
-    live = lax.broadcasted_iota(jnp.int32, (slots, LANES), 0) < counts_ref[0, 0]
+    live = lax.broadcasted_iota(jnp.int32, (slots, LANES), 0) < counts_ref[0, 0, 0]
     wanted = jnp.where(
         live, jnp.concatenate([picked_ref[0, j] for j in range(slots)], axis=0), -1
     )
@@ -353,19 +375,22 @@
     everyone = subs * crs
     last_rows[here] = jnp.sum(line, axis=0, keepdims=True)
 
-    def send_last(i, carry):
-        there = lax.rem(here + i, everyone)
+    def send_last(sub, core):
         pltpu.make_async_remote_copy(
             src_ref=last_rows.at[here],
             dst_ref=last_rows.at[here],
             send_sem=last_send_sem,
             recv_sem=last_sem,
-            device_id=(there // crs, lax.rem(there, crs)),
+            device_id=(sub, core),
             device_id_type=MESH,
         ).start()
-        return carry
-
-    lax.fori_loop(1, everyone, send_last, 0)
+
+    def send_last_to(sub):
+        send_last(sub, mine)
+        each_crs(lambda core: send_last(sub, core))
+
+    each_sub(send_last_to)
+    each_crs(lambda core: send_last(me, core))
     arrived = last_rows.at[pl.ds(0, everyone - 1)]
     pltpu.make_async_copy(arrived, arrived, last_sem).wait()
     whole = jnp.broadcast_to(jnp.sum(last_rows[...], axis=0), (8, LANES)) / all_rows
@@ -442,7 +467,7 @@
             pltpu.VMEM((coarse_rows, subs * kc), LOW),
             pltpu.SMEM((1, 1, slots), jnp.int32),
             pltpu.VMEM((1, slots, 1, block_rows), jnp.int32),
-            pltpu.SMEM((1, 1), jnp.int32),
+            pltpu.SMEM((1, 1, 1), jnp.int32),
             pltpu.VMEM((ROUNDS, 16, LANES), LOW),
             *[pltpu.VMEM((subs, 16, LANES), LOW) for number in range(ROUNDS)],
             pltpu.VMEM((SHARES, crs, 8, share_lanes), WIDE),
@@ -473,7 +498,7 @@
         coarse_inverse.reshape(coarse_rows, -1),
         neighbours,
         margin_rows.reshape(1, slots, 1, block_rows),
-        block_counts,
+        block_counts.reshape(1, 1, 1),
     )
     shape = (cols, 1, 1, rows)
     return both[0].reshape(shape), both[1].reshape(shape)

time: 36.4 us -> 35.3 us (0.970)
  Pallas kernels: 33.6 us -> 32.5 us
    pallas_call x1, Pallas kernels: 33.6 us -> 32.5 us  [body(): pl.pallas_call(functools.partial(kernel, sizes), out_shape=jax.ShapeDtype...]
where the time goes in v1:
time: 35.3 us; the launch traced here: 35.1 us
  Pallas kernels  32.5 us (92%)
  local copies, waits for them, and re-layouts  1.31 us (4%)
  between operations  1.29 us (4%)
    pallas_call x1, Pallas kernels, body(): pl.pallas_call(functools.partial(kernel, sizes), out_shape=jax.ShapeDtype...  32.5 us
    unnamed x1, local copies, waits for them, and re-layouts  1.31 us

profile of v1, /device:TPU:0, one launch (start us, length us, event | category | flops | bytes accessed | tf_op | source)
XLA Modules:
  0.0 35.1 jit_solution(15159438795511557639)
XLA Ops:
  1.3 32.5 %shard_map.104 = f32[2,4,1,384]{3,2,1,0:T(1,128)} custom-call(f32[4,1,384]{2,1,0:T(1,128)} %bitcast.20, bf16[384,384]{1,0:T(8,128)(2,1)} %bitcast.18, bf16[384,768]{1,0:T(8,128)(2,1)} %bitcast.17, bf16[384,1152]{1,0:T(8,128)(2,1)} %bitcast.16, f32[1,1,40,384]{3,2,1,0:T(8,128)} %basis_hbm.1, bf16[80,640]{1,0:T(8,128)(2,1)} %bitcast.19, ...), custom_call_target="tpu_custom_call" | custom-call | tf_op jit(solution)/shard_map/pallas_call | solution.py:456
  33.7 1.3 %slice_bitcast_fusion = (f32[4,1,1,384]{3,2,1,0:T(1,128)}, f32[4,1,1,384]{3,2,1,0:T(1,128)}) fusion(f32[2,4,1,384]{3,2,1,0:T(1,128)} %shard_map.104), kind=kLoop, calls=%fused_computation | loop fusion | bytes 24576

commit v2 on v1

--- a/solution.py
+++ b/solution.py
@@ -78,7 +78,6 @@
     last_rows,
     pick,
     coarse_wide,
-    placed,
     basis_parts,
     shifted,
     shifted_parts,
@@ -177,9 +176,13 @@
         return jnp.sum(a, axis=1, keepdims=True)
 
     def restrict(block):
-        parts = stack_parts(block)
-        both = nt(parts, basis_parts[0]) + nt(parts, basis_parts[1])
-        return both + swap_halves(both)
+        both = nt(stack_parts(block), basis_parts[...])
+        both = both + pltpu.roll(both, LANES // 2, 1)
+        both = jnp.where(lane_of < kc, both + swap_halves(both), 0.0)
+        moved = both
+        for t in range(1, together):
+            moved = jnp.where(lax.rem(me, together) == t, pltpu.roll(both, t * kc, 1), moved)
+        return moved
 
     def encode(value):
         high = value.astype(LOW).astype(WIDE)
@@ -237,13 +240,15 @@
             total = total + share[number, c]
         return total
 
-    def margin(number):
+    def fetch(number):
         lines = []
         for j in range(slots):
             tile = held[number][listed_ref[0, 0, j]].astype(WIDE)
             first = tile[:8]
             lines.append(jnp.concatenate([first, swap_halves(first), tile[8:]], axis=1))
-        fetched = nn(jnp.concatenate(lines, axis=0).astype(LOW), pick[...])
+        return nn(jnp.concatenate(lines, axis=0).astype(LOW), pick[...])
+
+    def margin(fetched):
         parts = [
             fetched[8 * j : 8 * j + 8, LANES * j : LANES * j + LANES] for j in range(slots)
         ]
@@ -270,16 +275,17 @@
 
     def prolong(total):
         parts = stack_parts(total)
-        both = nn(parts, shifted_parts[0]) + nn(parts, shifted_parts[1])
+        both = nn(jnp.concatenate([parts, parts], axis=1), shifted_parts[...])
         return both + pltpu.roll(both, 4, 0)
 
     def precondition(number, share_number, own_part):
         receive(number)
         sums = group_sums(number)
         solved = nt(jnp.concatenate(sums, axis=1).astype(LOW), coarse_wide[...])
+        fetched = fetch(number)
         totals = functools.reduce(jnp.add, sums)
         send_share(share_number, with_scalars(solved, totals))
-        fine = own_part + nt(margin(number), inverse_ref[:, rows:])
+        fine = own_part + nt(margin(fetched), inverse_ref[:, rows:])
         total = receive_share(share_number)
         return fine + prolong(total), swap_halves(total[:, :LANES])
 
@@ -289,12 +295,11 @@
         [right_ref[q] for q in range(cols)] + [jnp.zeros((8 - cols, rows), WIDE)], axis=0
     )
     basis = basis_ref[0, 0]
-    placed[...] = jnp.zeros_like(placed)
-    placed[pl.ds(pl.multiple_of(lax.rem(me, together) * kc, 8), kc), :] = basis
-    basis_full = placed[...]
-    basis_high = basis_full.astype(LOW)
-    basis_parts[0] = basis_high
-    basis_parts[1] = (basis_full - basis_high.astype(WIDE)).astype(LOW)
+    basis_high = basis.astype(LOW).astype(WIDE)
+    gap = jnp.zeros((LANES // 2 - kc, rows), WIDE)
+    basis_parts[...] = jnp.concatenate(
+        [basis_high, gap, basis - basis_high, gap], axis=0
+    ).astype(LOW)
     extra = restrict(right) + encode(row_sum(right * right))
     tile = pack(right, extra)
     held_0[me] = tile
@@ -316,8 +321,8 @@
     shifted[pl.ds(pl.multiple_of(mine * kc, 8), kc), :] = basis
     shifted_full = shifted[...]
     shifted_high = shifted_full.astype(LOW)
-    shifted_parts[0] = shifted_high
-    shifted_parts[1] = (shifted_full - shifted_high.astype(WIDE)).astype(LOW)
+    shifted_parts[:share_lanes] = shifted_high
+    shifted_parts[share_lanes:] = (shifted_full - shifted_high.astype(WIDE)).astype(LOW)
     loads[4].wait()
     coarse_rows = crs * kc
     coarse_cols = subs * kc
@@ -349,7 +354,7 @@
     loads[8].wait()
     own_part = nt(first_z.astype(LOW), own_ref[...])
     receive(1)
-    mapped = own_part + nt(margin(1), couple_ref[...])
+    mapped = own_part + nt(margin(fetch(1)), couple_ref[...])
 
     extra = restrict(mapped) + encode(row_sum(mapped * right))
     tile = pack(mapped, extra)
@@ -365,7 +370,7 @@
     own_part = nt(second_z.astype(LOW), own_ref[...])
     products = [row_sum(second * second), row_sum(right * second)]
     receive(3)
-    last = own_part + nt(margin(3), couple_ref[...])
+    last = own_part + nt(margin(fetch(3)), couple_ref[...])
 
     products = products + [row_sum(last * right), row_sum(last * second), row_sum(last * last)]
     line = jnp.zeros((8, LANES), WIDE)
@@ -455,7 +460,7 @@
     stays = pl.BlockSpec(memory_space=pltpu.HBM)
     both = pl.pallas_call(
         functools.partial(kernel, sizes),
-        out_shape=jax.ShapeDtypeStruct((2, cols, 1, rows), WIDE),
+        out_shape=pltpu.VMEM((2, cols, 1, rows), WIDE),
         in_specs=[stays] * 9,
         out_specs=vmem,
         scratch_shapes=[
@@ -474,10 +479,9 @@
             pltpu.VMEM((subs * crs, 1, LANES), WIDE),
             pltpu.VMEM((rows, slots * block_rows), LOW),
             pltpu.VMEM((share_lanes, groups * LANES), LOW),
-            pltpu.VMEM((LANES, rows), WIDE),
-            pltpu.VMEM((2, LANES, rows), LOW),
+            pltpu.VMEM((LANES, rows), LOW),
             pltpu.VMEM((share_lanes, rows), WIDE),
-            pltpu.VMEM((2, share_lanes, rows), LOW),
+            pltpu.VMEM((2 * share_lanes, rows), LOW),
             pltpu.SemaphoreType.DMA((9,)),
             pltpu.SemaphoreType.DMA,
             pltpu.SemaphoreType.DMA((ROUNDS,)),

time: 35.3 us -> 33.6 us (0.952)
  Pallas kernels: 32.5 us -> 31.5 us
  local copies, waits for them, and re-layouts: 1.31 us -> 0.6 us
    pallas_call x1, Pallas kernels: 32.5 us -> 31.5 us  [body(): pl.pallas_call(functools.partial(kernel, sizes), out_shape=pltpu.VMEM((2,...]
    unnamed x1, local copies, waits for them, and re-layouts: 1.31 us -> 0.6 us
where the time goes in v2:
time: 33.6 us; the launch traced here: 33.4 us
  Pallas kernels  31.5 us (94%)
  between operations  1.29 us (4%)
  local copies, waits for them, and re-layouts  0.6 us (2%)
    pallas_call x1, Pallas kernels, body(): pl.pallas_call(functools.partial(kernel, sizes), out_shape=pltpu.VMEM((2,...  31.5 us

profile of v2, /device:TPU:0, one launch (start us, length us, event | category | flops | bytes accessed | tf_op | source)
XLA Modules:
  0.0 33.4 jit_solution(2386123148392539193)
XLA Ops:
  1.3 31.5 %shard_map.104 = f32[2,4,1,384]{3,2,1,0:T(1,128)S(1)} custom-call(f32[4,1,384]{2,1,0:T(1,128)} %bitcast.20, bf16[384,384]{1,0:T(8,128)(2,1)} %bitcast.18, bf16[384,768]{1,0:T(8,128)(2,1)} %bitcast.17, bf16[384,1152]{1,0:T(8,128)(2,1)} %bitcast.16, f32[1,1,40,384]{3,2,1,0:T(8,128)} %basis_hbm.1, bf16[80,640]{1,0:T(8,128)(2,1)} %bitcast.19, ...), custom_call_target="tpu_custom_call" | custom-call | tf_op jit(solution)/shard_map/pallas_call | solution.py:461
  32.8 0.6 %slice_bitcast_fusion = (f32[4,1,1,384]{3,2,1,0:T(1,128)}, f32[4,1,1,384]{3,2,1,0:T(1,128)}) fusion(f32[2,4,1,384]{3,2,1,0:T(1,128)S(1)} %shard_map.104), kind=kLoop, calls=%fused_computation | loop fusion | bytes 24576

commit v3 on v2

--- a/solution.py
+++ b/solution.py
@@ -76,6 +76,9 @@
     held_3,
     share,
     last_rows,
+    own_t,
+    couple_t,
+    inverse_t,
     pick,
     coarse_wide,
     basis_parts,
@@ -172,6 +175,10 @@
     def nn(a, b):
         return jnp.dot(a, b, preferred_element_type=WIDE)
 
+    def turn(source, target):
+        for k in range(0, source.shape[1], LANES):
+            target[k : k + LANES, :] = source[:, k : k + LANES].T
+
     def row_sum(a):
         return jnp.sum(a, axis=1, keepdims=True)
 
@@ -285,7 +292,7 @@
         fetched = fetch(number)
         totals = functools.reduce(jnp.add, sums)
         send_share(share_number, with_scalars(solved, totals))
-        fine = own_part + nt(margin(fetched), inverse_ref[:, rows:])
+        fine = own_part + nn(margin(fetched), inverse_t[rows:])
         total = receive_share(share_number)
         return fine + prolong(total), swap_halves(total[:, :LANES])
 
@@ -342,7 +349,8 @@
         ).astype(LOW)
     loads[5].wait()
     loads[6].wait()
-    own_fine = nt(right.astype(LOW), inverse_ref[:, :rows])
+    turn(inverse_ref, inverse_t)
+    own_fine = nn(right.astype(LOW), inverse_t[:rows])
 
     first_z, totals = precondition(0, 0, own_fine)
     right_square = scalar(totals) / all_rows
@@ -352,25 +360,27 @@
     send(1, pack(first_z, nothing))
     loads[7].wait()
     loads[8].wait()
-    own_part = nt(first_z.astype(LOW), own_ref[...])
+    turn(own_ref, own_t)
+    turn(couple_ref, couple_t)
+    own_part = nn(first_z.astype(LOW), own_t[...])
     receive(1)
-    mapped = own_part + nt(margin(fetch(1)), couple_ref[...])
+    mapped = own_part + nn(margin(fetch(1)), couple_t[...])
 
     extra = restrict(mapped) + encode(row_sum(mapped * right))
     tile = pack(mapped, extra)
     held_2[me] = tile
     send(2, tile)
-    own_fine = nt(mapped.astype(LOW), inverse_ref[:, :rows])
+    own_fine = nn(mapped.astype(LOW), inverse_t[:rows])
     mapped_z, totals = precondition(2, 1, own_fine)
     height_11 = scalar(totals) / all_rows / (start * start)
     second_z = mapped_z - height_11 * first_z
     second = mapped - height_11 * right
 
     send(3, pack(second_z, nothing))
-    own_part = nt(second_z.astype(LOW), own_ref[...])
+    own_part = nn(second_z.astype(LOW), own_t[...])
     products = [row_sum(second * second), row_sum(right * second)]
     receive(3)
-    last = own_part + nt(margin(fetch(3)), couple_ref[...])
+    last = own_part + nn(margin(fetch(3)), couple_t[...])
 
     products = products + [row_sum(last * right), row_sum(last * second), row_sum(last * last)]
     line = jnp.zeros((8, LANES), WIDE)
@@ -477,6 +487,9 @@
             *[pltpu.VMEM((subs, 16, LANES), LOW) for number in range(ROUNDS)],
             pltpu.VMEM((SHARES, crs, 8, share_lanes), WIDE),
             pltpu.VMEM((subs * crs, 1, LANES), WIDE),
+            pltpu.VMEM((rows, rows), LOW),
+            pltpu.VMEM((slots * block_rows, rows), LOW),
+            pltpu.VMEM((rows + slots * block_rows, rows), LOW),
             pltpu.VMEM((rows, slots * block_rows), LOW),
             pltpu.VMEM((share_lanes, groups * LANES), LOW),
             pltpu.VMEM((LANES, rows), LOW),

time: 33.6 us -> 33.1 us (0.985)
  Pallas kernels: 31.5 us -> 31 us
    pallas_call x1, Pallas kernels: 31.5 us -> 31 us  [body(): pl.pallas_call(functools.partial(kernel, sizes), out_shape=pltpu.VMEM((2,...]
where the time goes in v3:
time: 33.1 us; the launch traced here: 32.9 us
  Pallas kernels  31 us (94%)
  between operations  1.29 us (4%)
  local copies, waits for them, and re-layouts  0.6 us (2%)
    pallas_call x1, Pallas kernels, body(): pl.pallas_call(functools.partial(kernel, sizes), out_shape=pltpu.VMEM((2,...  31 us

profile of v3, /device:TPU:0, one launch (start us, length us, event | category | flops | bytes accessed | tf_op | source)
XLA Modules:
  0.0 32.9 jit_solution(5705791526499710409)
XLA Ops:
  1.3 31.0 %shard_map.104 = f32[2,4,1,384]{3,2,1,0:T(1,128)S(1)} custom-call(f32[4,1,384]{2,1,0:T(1,128)} %bitcast.20, bf16[384,384]{1,0:T(8,128)(2,1)} %bitcast.18, bf16[384,768]{1,0:T(8,128)(2,1)} %bitcast.17, bf16[384,1152]{1,0:T(8,128)(2,1)} %bitcast.16, f32[1,1,40,384]{3,2,1,0:T(8,128)} %basis_hbm.1, bf16[80,640]{1,0:T(8,128)(2,1)} %bitcast.19, ...), custom_call_target="tpu_custom_call" | custom-call | tf_op jit(solution)/shard_map/pallas_call | solution.py:471
  32.3 0.6 %slice_bitcast_fusion = (f32[4,1,1,384]{3,2,1,0:T(1,128)}, f32[4,1,1,384]{3,2,1,0:T(1,128)}) fusion(f32[2,4,1,384]{3,2,1,0:T(1,128)S(1)} %shard_map.104), kind=kLoop, calls=%fused_computation | loop fusion | bytes 24576

commit v4 on v3

--- a/solution.py
+++ b/solution.py
@@ -77,7 +77,7 @@
     share,
     last_rows,
     own_t,
-    couple_t,
+    couple_wide,
     inverse_t,
     pick,
     coarse_wide,
@@ -247,19 +247,24 @@
             total = total + share[number, c]
         return total
 
-    def fetch(number):
+    def lines_of(number):
         lines = []
         for j in range(slots):
             tile = held[number][listed_ref[0, 0, j]].astype(WIDE)
             first = tile[:8]
             lines.append(jnp.concatenate([first, swap_halves(first), tile[8:]], axis=1))
-        return nn(jnp.concatenate(lines, axis=0).astype(LOW), pick[...])
-
-    def margin(fetched):
+        return lines
+
+    def margin(number):
+        fetched = nn(jnp.concatenate(lines_of(number), axis=0).astype(LOW), pick[...])
         parts = [
             fetched[8 * j : 8 * j + 8, LANES * j : LANES * j + LANES] for j in range(slots)
         ]
         return jnp.concatenate(parts, axis=1).astype(LOW)
+
+    def couple(number):
+        wide = jnp.concatenate(lines_of(number), axis=1).astype(LOW)
+        return nn(wide, couple_wide[...])
 
     def group_sums(number):
         sums = []
@@ -289,10 +294,9 @@
         receive(number)
         sums = group_sums(number)
         solved = nt(jnp.concatenate(sums, axis=1).astype(LOW), coarse_wide[...])
-        fetched = fetch(number)
         totals = functools.reduce(jnp.add, sums)
         send_share(share_number, with_scalars(solved, totals))
-        fine = own_part + nn(margin(fetched), inverse_t[rows:])
+        fine = own_part + nn(margin(number), inverse_t[rows:])
         total = receive_share(share_number)
         return fine + prolong(total), swap_halves(total[:, :LANES])
 
@@ -355,16 +359,21 @@
     first_z, totals = precondition(0, 0, own_fine)
     right_square = scalar(totals) / all_rows
     start = jnp.sqrt(right_square + EPSILON)
+    start_square_scale = 1.0 / (all_rows * (right_square + EPSILON))
 
     nothing = jnp.zeros((8, LANES), WIDE)
     send(1, pack(first_z, nothing))
     loads[7].wait()
     loads[8].wait()
     turn(own_ref, own_t)
-    turn(couple_ref, couple_t)
+    for j in range(slots):
+        block = slice(j * LANES, (j + 1) * LANES)
+        couple_wide[j * rows : (j + 1) * rows, :] = nt(
+            pick[:, block], couple_ref[:, block]
+        ).astype(LOW)
     own_part = nn(first_z.astype(LOW), own_t[...])
     receive(1)
-    mapped = own_part + nn(margin(fetch(1)), couple_t[...])
+    mapped = own_part + couple(1)
 
     extra = restrict(mapped) + encode(row_sum(mapped * right))
     tile = pack(mapped, extra)
@@ -372,7 +381,7 @@
     send(2, tile)
     own_fine = nn(mapped.astype(LOW), inverse_t[:rows])
     mapped_z, totals = precondition(2, 1, own_fine)
-    height_11 = scalar(totals) / all_rows / (start * start)
+    height_11 = scalar(totals) * start_square_scale
     second_z = mapped_z - height_11 * first_z
     second = mapped - height_11 * right
 
@@ -380,7 +389,7 @@
     own_part = nn(second_z.astype(LOW), own_t[...])
     products = [row_sum(second * second), row_sum(right * second)]
     receive(3)
-    last = own_part + nn(margin(fetch(3)), couple_t[...])
+    last = own_part + couple(3)
 
     products = products + [row_sum(last * right), row_sum(last * second), row_sum(last * last)]
     line = jnp.zeros((8, LANES), WIDE)
@@ -488,7 +497,7 @@
             pltpu.VMEM((SHARES, crs, 8, share_lanes), WIDE),
             pltpu.VMEM((subs * crs, 1, LANES), WIDE),
             pltpu.VMEM((rows, rows), LOW),
-            pltpu.VMEM((slots * block_rows, rows), LOW),
+            pltpu.VMEM((slots * rows, rows), LOW),
             pltpu.VMEM((rows + slots * block_rows, rows), LOW),
             pltpu.VMEM((rows, slots * block_rows), LOW),
             pltpu.VMEM((share_lanes, groups * LANES), LOW),

time: 33.1 us -> 33.7 us (1.018)
  Pallas kernels: 31 us -> 31.6 us
    pallas_call x1, Pallas kernels: 31 us -> 31.6 us  [body(): pl.pallas_call(functools.partial(kernel, sizes), out_shape=pltpu.VMEM((2,...]
where the time goes in v4:
time: 33.7 us; the launch traced here: 33.5 us
  Pallas kernels  31.6 us (94%)
  between operations  1.29 us (4%)
  local copies, waits for them, and re-layouts  0.6 us (2%)
    pallas_call x1, Pallas kernels, body(): pl.pallas_call(functools.partial(kernel, sizes), out_shape=pltpu.VMEM((2,...  31.6 us

profile of v4, /device:TPU:0, one launch (start us, length us, event | category | flops | bytes accessed | tf_op | source)
XLA Modules:
  0.0 33.5 jit_solution(8677009640543495944)
XLA Ops:
  1.3 31.6 %shard_map.104 = f32[2,4,1,384]{3,2,1,0:T(1,128)S(1)} custom-call(f32[4,1,384]{2,1,0:T(1,128)} %bitcast.20, bf16[384,384]{1,0:T(8,128)(2,1)} %bitcast.18, bf16[384,768]{1,0:T(8,128)(2,1)} %bitcast.17, bf16[384,1152]{1,0:T(8,128)(2,1)} %bitcast.16, f32[1,1,40,384]{3,2,1,0:T(8,128)} %basis_hbm.1, bf16[80,640]{1,0:T(8,128)(2,1)} %bitcast.19, ...), custom_call_target="tpu_custom_call" | custom-call | tf_op jit(solution)/shard_map/pallas_call | solution.py:480
  32.8 0.6 %slice_bitcast_fusion = (f32[4,1,1,384]{3,2,1,0:T(1,128)}, f32[4,1,1,384]{3,2,1,0:T(1,128)}) fusion(f32[2,4,1,384]{3,2,1,0:T(1,128)S(1)} %shard_map.104), kind=kLoop, calls=%fused_computation | loop fusion | bytes 24576

commit v5 on v3

--- a/solution.py
+++ b/solution.py
@@ -101,46 +101,6 @@
     lane_of = lax.broadcasted_iota(jnp.int32, (8, LANES), 1)
     top = row_of < 4
 
-    barrier = pltpu.get_barrier_semaphore()
-
-    short = subs & (subs - 1) == 0 and subs <= 16
-
-    def flipped(index, mask, bits):
-        moved = index
-        for k in range(bits):
-            if mask >> k & 1:
-                moved = moved + (1 << k) - (index // (1 << k)) % 2 * (2 << k)
-        return moved
-
-    def each_sub(act):
-        if short:
-            for mask in ORDER:
-                if mask < subs:
-                    act(flipped(me, mask, 4))
-        else:
-
-            def one(i, carry):
-                act(lax.rem(me + i, subs))
-                return carry
-
-            lax.fori_loop(1, subs, one, 0)
-
-    def each_crs(act):
-        def one(i, carry):
-            act(lax.rem(mine + i, crs))
-            return carry
-
-        if crs == 2:
-            act(1 - mine)
-        else:
-            lax.fori_loop(1, crs, one, 0)
-
-    def greet(sub, core):
-        pl.semaphore_signal(barrier, inc=1, device_id=(sub, core), device_id_type=MESH)
-
-    each_sub(lambda sub: greet(sub, mine))
-    each_crs(lambda core: greet(me, core))
-
     pairs = [
         (right_hbm, right_ref),
         (basis_hbm, basis_ref),
@@ -156,7 +116,49 @@
         pltpu.make_async_copy(there, here, load_sems.at[n])
         for n, (there, here) in enumerate(pairs)
     ]
-    for load in loads:
+    loads[0].start()
+    loads[1].start()
+    barrier = pltpu.get_barrier_semaphore()
+
+    short = subs & (subs - 1) == 0 and subs <= 16
+
+    def flipped(index, mask, bits):
+        moved = index
+        for k in range(bits):
+            if mask >> k & 1:
+                moved = moved + (1 << k) - (index // (1 << k)) % 2 * (2 << k)
+        return moved
+
+    def each_sub(act):
+        if short:
+            for mask in ORDER:
+                if mask < subs:
+                    act(flipped(me, mask, 4))
+        else:
+
+            def one(i, carry):
+                act(lax.rem(me + i, subs))
+                return carry
+
+            lax.fori_loop(1, subs, one, 0)
+
+    def each_crs(act):
+        def one(i, carry):
+            act(lax.rem(mine + i, crs))
+            return carry
+
+        if crs == 2:
+            act(1 - mine)
+        else:
+            lax.fori_loop(1, crs, one, 0)
+
+    def greet(sub, core):
+        pl.semaphore_signal(barrier, inc=1, device_id=(sub, core), device_id_type=MESH)
+
+    each_sub(lambda sub: greet(sub, mine))
+    each_crs(lambda core: greet(me, core))
+
+    for load in loads[2:]:
         load.start()
 
     def swap_halves(block):
@@ -289,10 +291,9 @@
         receive(number)
         sums = group_sums(number)
         solved = nt(jnp.concatenate(sums, axis=1).astype(LOW), coarse_wide[...])
-        fetched = fetch(number)
         totals = functools.reduce(jnp.add, sums)
         send_share(share_number, with_scalars(solved, totals))
-        fine = own_part + nn(margin(fetched), inverse_t[rows:])
+        fine = own_part + nn(margin(fetch(number)), inverse_t[rows:])
         total = receive_share(share_number)
         return fine + prolong(total), swap_halves(total[:, :LANES])
 
@@ -355,6 +356,7 @@
     first_z, totals = precondition(0, 0, own_fine)
     right_square = scalar(totals) / all_rows
     start = jnp.sqrt(right_square + EPSILON)
+    start_square_scale = 1.0 / (all_rows * (right_square + EPSILON))
 
     nothing = jnp.zeros((8, LANES), WIDE)
     send(1, pack(first_z, nothing))
@@ -372,7 +374,7 @@
     send(2, tile)
     own_fine = nn(mapped.astype(LOW), inverse_t[:rows])
     mapped_z, totals = precondition(2, 1, own_fine)
-    height_11 = scalar(totals) / all_rows / (start * start)
+    height_11 = scalar(totals) * start_square_scale
     second_z = mapped_z - height_11 * first_z
     second = mapped - height_11 * right
 

time: 33.1 us -> 33.5 us (1.012)
  Pallas kernels: 31 us -> 31.4 us
    pallas_call x1, Pallas kernels: 31 us -> 31.4 us  [body(): pl.pallas_call(functools.partial(kernel, sizes), out_shape=pltpu.VMEM((2,...]
where the time goes in v5:
time: 33.5 us; the launch traced here: 33.3 us
  Pallas kernels  31.4 us (94%)
  between operations  1.29 us (4%)
  local copies, waits for them, and re-layouts  0.6 us (2%)
    pallas_call x1, Pallas kernels, body(): pl.pallas_call(functools.partial(kernel, sizes), out_shape=pltpu.VMEM((2,...  31.4 us

profile of v5, /device:TPU:0, one launch (start us, length us, event | category | flops | bytes accessed | tf_op | source)
XLA Modules:
  0.0 33.3 jit_solution(4336804513149282855)
XLA Ops:
  1.3 31.4 %shard_map.104 = f32[2,4,1,384]{3,2,1,0:T(1,128)S(1)} custom-call(f32[4,1,384]{2,1,0:T(1,128)} %bitcast.20, bf16[384,384]{1,0:T(8,128)(2,1)} %bitcast.18, bf16[384,768]{1,0:T(8,128)(2,1)} %bitcast.17, bf16[384,1152]{1,0:T(8,128)(2,1)} %bitcast.16, f32[1,1,40,384]{3,2,1,0:T(8,128)} %basis_hbm.1, bf16[80,640]{1,0:T(8,128)(2,1)} %bitcast.19, ...), custom_call_target="tpu_custom_call" | custom-call | tf_op jit(solution)/shard_map/pallas_call | solution.py:473
  32.7 0.6 %slice_bitcast_fusion = (f32[4,1,1,384]{3,2,1,0:T(1,128)}, f32[4,1,1,384]{3,2,1,0:T(1,128)}) fusion(f32[2,4,1,384]{3,2,1,0:T(1,128)S(1)} %shard_map.104), kind=kLoop, calls=%fused_computation | loop fusion | bytes 24576

commit v6 on v3

--- a/solution.py
+++ b/solution.py
@@ -292,7 +292,10 @@
         fetched = fetch(number)
         totals = functools.reduce(jnp.add, sums)
         send_share(share_number, with_scalars(solved, totals))
-        fine = own_part + nn(margin(fetched), inverse_t[rows:])
+        if number:
+            fine = own_part + nn(margin(fetched), inverse_t[rows:])
+        else:
+            fine = own_part + nt(margin(fetched), inverse_ref[:, rows:])
         total = receive_share(share_number)
         return fine + prolong(total), swap_halves(total[:, :LANES])
 
@@ -349,8 +352,7 @@
         ).astype(LOW)
     loads[5].wait()
     loads[6].wait()
-    turn(inverse_ref, inverse_t)
-    own_fine = nn(right.astype(LOW), inverse_t[:rows])
+    own_fine = nt(right.astype(LOW), inverse_ref[:, :rows])
 
     first_z, totals = precondition(0, 0, own_fine)
     right_square = scalar(totals) / all_rows
@@ -370,6 +372,7 @@
     tile = pack(mapped, extra)
     held_2[me] = tile
     send(2, tile)
+    turn(inverse_ref, inverse_t)
     own_fine = nn(mapped.astype(LOW), inverse_t[:rows])
     mapped_z, totals = precondition(2, 1, own_fine)
     height_11 = scalar(totals) / all_rows / (start * start)

time: 33.1 us -> 33.3 us (level)
  no operation moved by 1% of the time
where the time goes in v6:
time: 33.3 us; the launch traced here: 33.1 us
  Pallas kernels  31.2 us (94%)
  between operations  1.29 us (4%)
  local copies, waits for them, and re-layouts  0.6 us (2%)
    pallas_call x1, Pallas kernels, body(): pl.pallas_call(functools.partial(kernel, sizes), out_shape=pltpu.VMEM((2,...  31.2 us

profile of v6, /device:TPU:0, one launch (start us, length us, event | category | flops | bytes accessed | tf_op | source)
XLA Modules:
  0.0 33.1 jit_solution(13948342145336735546)
XLA Ops:
  1.3 31.2 %shard_map.104 = f32[2,4,1,384]{3,2,1,0:T(1,128)S(1)} custom-call(f32[4,1,384]{2,1,0:T(1,128)} %bitcast.20, bf16[384,384]{1,0:T(8,128)(2,1)} %bitcast.18, bf16[384,768]{1,0:T(8,128)(2,1)} %bitcast.17, bf16[384,1152]{1,0:T(8,128)(2,1)} %bitcast.16, f32[1,1,40,384]{3,2,1,0:T(8,128)} %basis_hbm.1, bf16[80,640]{1,0:T(8,128)(2,1)} %bitcast.19, ...), custom_call_target="tpu_custom_call" | custom-call | tf_op jit(solution)/shard_map/pallas_call | solution.py:474
  32.5 0.6 %slice_bitcast_fusion = (f32[4,1,1,384]{3,2,1,0:T(1,128)}, f32[4,1,1,384]{3,2,1,0:T(1,128)}) fusion(f32[2,4,1,384]{3,2,1,0:T(1,128)S(1)} %shard_map.104), kind=kLoop, calls=%fused_computation | loop fusion | bytes 24576

commit v7 on v3

--- a/solution.py
+++ b/solution.py
@@ -12,7 +12,7 @@
 LANES = 128
 ROUNDS = 4
 SHARES = 2
-ORDER = (15, 11, 14, 13, 10, 9, 12, 8, 7, 6, 5, 4, 3, 2, 1)
+ORDER = (15, 7, 11, 3, 14, 6, 13, 5, 10, 2, 9, 1, 12, 4, 8)
 AT = 120
 NT = (((1,), (1,)), ((), ()))
 LOW = jnp.bfloat16

time: 33.1 us -> 32.9 us (level)
  no operation moved by 1% of the time
where the time goes in v7:
time: 32.9 us; the launch traced here: 32.7 us
  Pallas kernels  30.8 us (94%)
  between operations  1.29 us (4%)
  local copies, waits for them, and re-layouts  0.6 us (2%)
    pallas_call x1, Pallas kernels, body(): pl.pallas_call(functools.partial(kernel, sizes), out_shape=pltpu.VMEM((2,...  30.8 us

profile of v7, /device:TPU:0, one launch (start us, length us, event | category | flops | bytes accessed | tf_op | source)
XLA Modules:
  0.0 32.7 jit_solution(792740715402200687)
XLA Ops:
  1.3 30.8 %shard_map.104 = f32[2,4,1,384]{3,2,1,0:T(1,128)S(1)} custom-call(f32[4,1,384]{2,1,0:T(1,128)} %bitcast.20, bf16[384,384]{1,0:T(8,128)(2,1)} %bitcast.18, bf16[384,768]{1,0:T(8,128)(2,1)} %bitcast.17, bf16[384,1152]{1,0:T(8,128)(2,1)} %bitcast.16, f32[1,1,40,384]{3,2,1,0:T(8,128)} %basis_hbm.1, bf16[80,640]{1,0:T(8,128)(2,1)} %bitcast.19, ...), custom_call_target="tpu_custom_call" | custom-call | tf_op jit(solution)/shard_map/pallas_call | solution.py:471
  32.1 0.6 %slice_bitcast_fusion = (f32[4,1,1,384]{3,2,1,0:T(1,128)}, f32[4,1,1,384]{3,2,1,0:T(1,128)}) fusion(f32[2,4,1,384]{3,2,1,0:T(1,128)S(1)} %shard_map.104), kind=kLoop, calls=%fused_computation | loop fusion | bytes 24576
